TPU v7x, 32 devices: a whole 2x2x4 slice. The times are simulated.
32 devices in a mesh: region: 4 (over y, core), cols: 8 (over z, x).
Axes of the slice: x: 2, y: 2, z: 4, core: 2. Of those that a mesh axis runs over, the one named last changes fastest.
Arguments:
- incidence: bfloat16 [4, 8, 8, 128, 1024], P('region', 'cols'), may hold values from 0 to 1, as said below
- tile_rows: int32 [4, 8, 8], P('region', 'cols'), may hold values from 0 to 63, as said below
- tile_cols: int32 [4, 8, 8], P('region', 'cols'), may hold values from 0 to 63, as said below
- tile_count: int32 [4, 8], P('region', 'cols'), may hold values from 1 to 8, as said below
- route_cost: float32 [524288], P('cols'), may hold values from 1 to 18
- primal: float32 [524288], P('cols'), may hold values from 0 to 1
- duals: float32 [32768], P('region'), may hold values from -6 to 6
- balance: float32 [], replicated, may hold values from 0.2 to 0.8
Outputs:
- primal_next: float32 [524288], P('cols')
- duals_next: float32 [32768], P('region')
- balance_next: float32 [], replicated
Inputs may be any that keep to these rules, and one draw needn't show every extreme that they name: `incidence`: entries are 0 or 1. On one device the (tile_rows, tile_cols) pairs of its slots are distinct. On one device the (tile_rows, tile_cols) pairs of its slots are distinct. Slots from tile_count on hold no part of A; on every region index some device has all 8 slots live.
All inputs are finite; a program needn't handle non-finite values.
Results may differ from a plain program's by a relative error of at most 0.0003.
Values sent between devices are 32-bit elements; how exact they have to be, the bound alone decides.
A program may use at most 64 MiB of HBM per device.

v0:
```python
import jax
import jax.numpy as jnp
from jax import lax
from jax.sharding import PartitionSpec as P

ITERS = 2


step_scale = 0.012
epsilon = 1e-06
highest = lax.Precision.HIGHEST


def local(incidence, tile_rows, tile_cols, tile_count, route_cost, primal, duals, balance):
    slots = incidence.shape[2]
    tile_height = incidence.shape[3]
    tile_width = incidence.shape[4]
    blocks = incidence.reshape(slots, tile_height, tile_width)
    slot_rows = tile_rows.reshape(slots)
    slot_cols = tile_cols.reshape(slots)
    live_slots = jnp.arange(slots, dtype=jnp.int32) < tile_count.reshape(())
    row_blocks = duals.shape[0] // tile_height
    col_blocks = primal.shape[0] // tile_width
    row_pick = (
        (slot_rows[:, None] == jnp.arange(row_blocks, dtype=jnp.int32)[None, :])
        & live_slots[:, None]
    ).astype(jnp.float32)
    col_pick = (
        (slot_cols[:, None] == jnp.arange(col_blocks, dtype=jnp.int32)[None, :])
        & live_slots[:, None]
    ).astype(jnp.float32)
    for iteration in range(ITERS):
        primal_step = step_scale / balance
        dual_step = step_scale * balance
        dual_rows = duals.reshape(row_blocks, tile_height)[slot_rows]
        column_products = jnp.einsum(
            "sij,si->sj", blocks, dual_rows, precision=highest, preferred_element_type=jnp.float32
        )
        col_terms = jnp.einsum("sb,sj->bj", col_pick, column_products, precision=highest).reshape(
            -1
        )
        col_total = lax.psum(col_terms, "region")
        moved = jnp.clip(primal - primal_step * (route_cost - col_total), 0.0, 1.0)
        primal_moves = jnp.sum((moved - primal) ** 2)
        extrapolated = 2.0 * moved - primal
        primal_cols = extrapolated.reshape(col_blocks, tile_width)[slot_cols]
        products = jnp.einsum(
            "sij,sj->si", blocks, primal_cols, precision=highest, preferred_element_type=jnp.float32
        )
        coverage = lax.psum(
            jnp.einsum("sr,si->ri", row_pick, products, precision=highest).reshape(-1), "cols"
        )
        updated = duals + dual_step * (1.0 - coverage)
        dual_moves = jnp.sum((updated - duals) ** 2)
        primal_total = lax.psum(primal_moves, "cols")
        dual_total = lax.psum(dual_moves, "region")
        balance = jnp.sqrt(balance * jnp.sqrt((dual_total + epsilon) / (primal_total + epsilon)))
        primal = moved
        duals = updated
    return (primal, duals, balance)


def solution(mesh):
    return jax.shard_map(
        local,
        mesh=mesh,
        in_specs=(
            P("region", "cols", None, None, None),
            P("region", "cols", None),
            P("region", "cols", None),
            P("region", "cols"),
            P("cols"),
            P("cols"),
            P("region"),
            P(),
        ),
        out_specs=(P("cols"), P("region"), P()),
        check_vma=False,
    )
```

profile of v0, /device:TPU:0, one launch (start us, length us, event | category | flops | bytes accessed | tf_op | source)
XLA Modules:
  0.0 181.5 jit_solution(10237958210254005699)
XLA Ops:
  7.2 0.0 copy-start
  7.2 0.0 copy-start.5
  7.2 0.0 copy-start.2
  7.2 0.0 copy-start.1
  7.2 0.0 all-reduce.5.cloned.1.call-start
  8.1 0.7 fusion.28
  8.7 1.3 gather_fusion
  10.0 0.0 copy-done
  10.1 0.9 fusion.6
  11.0 0.0 copy-done.5
  11.0 0.4 convolution_bitcast_fusion.1
  11.4 0.8 copy.19
  12.1 0.0 all-reduce.5.cloned.1.call-update
  12.2 0.0 all-reduce.7.cloned.1.call-start
  12.9 34.1 %all-reduce.5.cloned.1.call-done = f32[65536]{0:T(1024)} async-done(((f32[65536]{0:T(1024)}), f32[65536]{0:T(1024)}) %all-reduce.5.cloned.1.call-update) | async-done | bytes 262160 | tf_op jit(solution)/shard_map/psum | solution.py:42
  47.0 0.0 copy-done.2
  47.0 0.0 copy-done.1
  47.0 1.6 multiply_reduce_fusion.1
  48.6 0.0 copy-start.6
  48.6 0.0 copy-start.4
  48.7 0.6 gather_fusion.1
  49.3 1.7 fusion.4
  51.0 0.0 copy-done.6
  51.0 0.3 convolution_bitcast_fusion.3
  51.3 38.6 %all-reduce.1 = (f32[8192]{0:T(1024)S(1)}, f32[]{:T(128)}) all-reduce(f32[8192]{0:T(1024)S(1)} %convolution_bitcast_fusion.3, f32[]{:T(128)} %get-tuple-element.13), channel_id=1, replica_groups=mesh['region'=4,'cols'=8] {'cols'}, use_global_device_ids=true, to_apply=%region_1.2 | all-reduce | flops 8193 | bytes 65544 | tf_op jit(solution)/shard_map/psum | solution.py:50
  89.9 0.0 copy-done.4
  89.9 0.6 multiply_reduce_fusion.3
  90.5 0.6 gather_fusion.2
  91.1 0.9 fusion.2
  92.0 0.4 convolution_bitcast_fusion
  92.4 0.8 copy.20
  93.1 0.0 all-reduce.7.cloned.1.call-update
  93.1 6.5 %psum.58 = f32[]{:T(128)} all-reduce(f32[]{:T(128)} %get-tuple-element.11), channel_id=1, replica_groups=mesh['region'=4,'cols'=8] {'region'}, use_global_device_ids=true, to_apply=%region_3.4 | all-reduce | flops 1 | bytes 8 | tf_op jit(solution)/shard_map/psum | solution.py:56
  101.1 20.4 %all-reduce.7.cloned.1.call-done = f32[65536]{0:T(1024)} async-done(((f32[65536]{0:T(1024)}), f32[65536]{0:T(1024)}) %all-reduce.7.cloned.1.call-update) | async-done | bytes 262160 | tf_op jit(solution)/shard_map/psum | solution.py:42
  121.5 1.6 multiply_reduce_fusion
  123.1 0.0 copy-start.3
  123.2 0.6 gather_fusion.3
  123.8 1.7 fusion
  125.5 0.3 convolution_bitcast_fusion.2
  125.8 38.6 %all-reduce = (f32[8192]{0:T(1024)S(1)}, f32[]{:T(128)}) all-reduce(f32[8192]{0:T(1024)S(1)} %convolution_bitcast_fusion.2, f32[]{:T(128)} %get-tuple-element.9), channel_id=1, replica_groups=mesh['region'=4,'cols'=8] {'cols'}, use_global_device_ids=true, to_apply=%region_7.8 | all-reduce | flops 8193 | bytes 65544 | tf_op jit(solution)/shard_map/psum | solution.py:50
  164.4 1.3 multiply_reduce_fusion.2
  165.7 6.5 %psum.62 = f32[]{:T(128)} all-reduce(f32[]{:T(128)} %get-tuple-element.7), channel_id=1, replica_groups=mesh['region'=4,'cols'=8] {'region'}, use_global_device_ids=true, to_apply=%region_9.10 | all-reduce | flops 1 | bytes 8 | tf_op jit(solution)/shard_map/psum | solution.py:56
  173.5 0.0 copy-done.3
  (8 shorter events, 0.2 us)
Async XLA Ops:
  7.2 2.9 %copy-start = (bf16[1,1,8,128,1024]{4,3,2,1,0:T(8,128)(2,1)S(1)}, bf16[1,1,8,128,1024]{4,3,2,1,0:T(8,128)(2,1)}, u32[]{:S(2)}) copy-start(bf16[1,1,8,128,1024]{4,3,2,1,0:T(8,128)(2,1)} %param.8) | copy-start | bytes 6291460
  7.2 3.8 %copy-start.5 = (s32[1,1,8]{2,1,0:T(1,128)S(1)}, s32[1,1,8]{2,1,0:T(1,128)}, u32[]{:S(2)}) copy-start(s32[1,1,8]{2,1,0:T(1,128)} %param.10) | copy-start | bytes 100
  7.2 39.8 %copy-start.2 = (f32[65536]{0:T(1024)S(1)}, f32[65536]{0:T(1024)}, u32[]{:S(2)}) copy-start(f32[65536]{0:T(1024)} %param.12) | copy-start | bytes 786436
  7.2 39.8 %copy-start.1 = (f32[65536]{0:T(1024)S(1)}, f32[65536]{0:T(1024)}, u32[]{:S(2)}) copy-start(f32[65536]{0:T(1024)} %param.13) | copy-start | bytes 786436
  7.2 39.8 %all-reduce.5.cloned.1.call-start = ((), (), s32[]{:S(2)}) async-start(), calls=%async_computation | async-start | bytes 524288 | tf_op jit(solution)/shard_map/psum | solution.py:42
  12.2 109.4 %all-reduce.7.cloned.1.call-start = ((), (), s32[]{:S(2)}) async-start(), calls=%async_computation.1 | async-start | bytes 524288 | tf_op jit(solution)/shard_map/psum | solution.py:42
  48.6 2.4 %copy-start.6 = (s32[1,1,8]{2,1,0:T(1,128)S(1)}, s32[1,1,8]{2,1,0:T(1,128)}, u32[]{:S(2)}) copy-start(s32[1,1,8]{2,1,0:T(1,128)} %param.9) | copy-start | bytes 100
  48.6 41.3 %copy-start.4 = (f32[8192]{0:T(1024)S(1)}, f32[8192]{0:T(1024)}, u32[]{:S(2)}) copy-start(f32[8192]{0:T(1024)} %param.14) | copy-start | bytes 98308
  123.1 50.4 %copy-start.3 = (f32[65536]{0:T(1024)}, f32[65536]{0:T(1024)S(1)}, u32[]{:S(2)}) copy-start(f32[65536]{0:T(1024)S(1)} %get-tuple-element.10) | copy-start | bytes 786436
Sparse Core Ops, SparseCore 0:
  12.3 34.6 all-reduce.4
  93.3 28.1 all-reduce.6
where the time goes:
time: 182 us; the launch traced here: 181 us
  blocking collectives  90.1 us (50%)
  waiting for transfers between devices  54.5 us (30%)
  between operations  19.6 us (11%)
  matrix products  6.67 us (4%)
  other arithmetic  5.9 us (3%)
  local copies, waits for them, and re-layouts  4.63 us (3%)
    psum x2, blocking collectives, local(): lax.psum(jnp.einsum('sr,si->ri', row_pick, products, precision=highest).r...  77.2 us
    psum x2, waiting for transfers between devices, local(): col_total = lax.psum(col_terms, 'region')  54.5 us
    psum x2, blocking collectives, local(): dual_total = lax.psum(dual_moves, 'region')  12.9 us
  transfers between devices with their start and end apart: 2, of which 2 were waited for; matrix products, arithmetic and copies ran while one was open for 0% of the time, Pallas kernels for 0%

commit v1 on v0

v1 whole, which is shorter than its diff:
```python
import functools

import jax
import jax.numpy as jnp
from jax import lax
from jax.experimental import pallas as pl
from jax.experimental.pallas import tpu as pltpu
from jax.sharding import PartitionSpec as P

ITERS = 2

step_scale = 0.012
epsilon = 1e-06
MESH = pl.DeviceIdType.MESH
LANES = 128
SUB = 8


def split(value):
    high = value.astype(jnp.bfloat16).astype(jnp.float32)
    rest = value - high
    middle = rest.astype(jnp.bfloat16).astype(jnp.float32)
    return high, middle, rest - middle


def stacked(value):
    high, middle, low = split(value)
    rows = jnp.concatenate([high, middle, low, jnp.zeros_like(value)], axis=0)
    return rows.astype(jnp.bfloat16)


def unstacked(product):
    return product[2 * SUB : 3 * SUB] + product[SUB : 2 * SUB] + product[:SUB]


def scatter(picks, blocks):
    sides = [term.astype(jnp.bfloat16) for term in split(blocks)]
    product = jnp.dot(
        picks, jnp.concatenate(sides, axis=1), preferred_element_type=jnp.float32
    )
    return product[:, 2 * LANES :] + product[:, LANES : 2 * LANES] + product[:, :LANES]


def folded(value):
    return jnp.sum(value.reshape(-1, SUB, LANES), axis=0)


def kernel(
    regions, groups,
    tile_rows, tile_cols, tile_count, balance,
    incidence_hbm, cost_hbm, primal_hbm, duals_hbm,
    primal_out, duals_out, balance_out,
    tiles, cost, x, y, extrapolated, dual_rows, primal_cols,
    col_picks, row_picks, col_box, row_box, last_box,
    load_sem, store_sem,
    col_send, col_recv, row_send, row_recv, last_send, last_recv,
):
    region, group = lax.axis_index("region"), lax.axis_index("cols")
    width = tiles.shape[1]
    chunks = width // LANES

    loads = [
        pltpu.make_async_copy(source, target, load_sem.at[i])
        for i, (source, target) in enumerate(
            ((duals_hbm, y), (incidence_hbm, tiles), (primal_hbm, x), (cost_hbm, cost))
        )
    ]
    for load in loads:
        load.start()

    region_peers = [lax.rem(region + d, regions) for d in range(1, regions)]
    group_peers = [lax.rem(group + d, groups) for d in range(1, groups)]
    barrier = pltpu.get_barrier_semaphore()
    for peer in region_peers:
        pl.semaphore_signal(barrier, inc=1, device_id=(peer, group), device_id_type=MESH)
    for peer in group_peers:
        pl.semaphore_signal(barrier, inc=1, device_id=(region, peer), device_id_type=MESH)

    def region_copy(box, send, recv, owner, peer, send_slot):
        return pltpu.make_async_remote_copy(
            src_ref=box.at[owner], dst_ref=box.at[owner],
            send_sem=send.at[send_slot], recv_sem=recv.at[owner],
            device_id=(peer, group), device_id_type=MESH,
        )

    def group_copy(box, send, recv, owner, peer, send_slot):
        return pltpu.make_async_remote_copy(
            src_ref=box.at[owner], dst_ref=box.at[owner],
            send_sem=send.at[send_slot], recv_sem=recv.at[owner],
            device_id=(region, peer), device_id_type=MESH,
        )

    pending = []

    def exchange(copy, me, peers, box, send, recv):
        for slot, peer in enumerate(peers):
            sent = copy(box, send, recv, me, peer, slot)
            sent.start()
            pending.append(sent)

    def arrive(copy, peers, box, send, recv):
        for slot, peer in enumerate(peers):
            copy(box, send, recv, peer, peer, slot).wait_recv()

    lane = lax.broadcasted_iota(jnp.int32, (SUB, LANES), 1)
    sub = lax.broadcasted_iota(jnp.int32, (SUB, LANES), 0)
    rows_of, cols_of = [], []
    col_marks = jnp.full((SUB, LANES), -1, jnp.int32)
    row_marks = jnp.full((SUB, LANES), -1, jnp.int32)
    for s in range(SUB):
        rows_of.append(tile_rows[0, 0, s])
        cols_of.append(tile_cols[0, 0, s])
        mine = jnp.logical_and(lane % SUB == s, s < jnp.full((SUB, LANES), tile_count[0, 0]))
        col_marks = jnp.where(mine, cols_of[s] * chunks + (lane // SUB) % chunks, col_marks)
        row_marks = jnp.where(mine, rows_of[s], row_marks)

    weight = jnp.full((1, 1), balance[0], jnp.float32)
    half = SUB * chunks
    pl.semaphore_wait(barrier, regions + groups - 2)

    for iteration in range(ITERS):
        cbox, csend, crecv = col_box.at[iteration], col_send.at[iteration], col_recv.at[iteration]
        rbox, rsend, rrecv = row_box.at[iteration], row_send.at[iteration], row_recv.at[iteration]
        dual_step = step_scale * weight

        if iteration == 0:
            loads[0].wait()
        for s in range(SUB):
            dual_rows[s] = y[rows_of[s]]
        picked = dual_rows[...]
        diagonal = jnp.concatenate([jnp.where(sub == s, picked, 0.0) for s in range(SUB)], axis=1)
        if iteration == 0:
            loads[1].wait()
        products = unstacked(
            jnp.dot(stacked(diagonal), tiles[...], preferred_element_type=jnp.float32)
        )
        for k in range(chunks):
            cbox[region, k * SUB : (k + 1) * SUB, :] = products[:, k * LANES : (k + 1) * LANES]
        if iteration == 0:
            cbox[region, half : half + SUB, :] = col_marks.astype(jnp.float32)
        else:
            cbox[region, half : half + SUB, :] = dual_moves
        exchange(region_copy, region, region_peers, cbox, csend, crecv)
        if iteration == 0:
            loads[2].wait()
            loads[3].wait()
        arrive(region_copy, region_peers, cbox, csend, crecv)

        if iteration == 0:
            place = lax.broadcasted_iota(jnp.int32, (x.shape[0], LANES), 0).astype(jnp.float32)
            spot = lax.broadcasted_iota(jnp.int32, (1, LANES), 1)
            per = LANES // half
            for j in range(regions // per):
                marks = cbox[j * per, half : half + 1, :]
                for i in range(1, per):
                    marks = jnp.where(spot // half == i, cbox[j * per + i, half : half + 1, :], marks)
                col_picks[:, j * LANES : (j + 1) * LANES] = jnp.where(
                    place == marks, 1.0, 0.0
                ).astype(jnp.bfloat16)
        else:
            dual_total = cbox[0, half : half + SUB, :]
            for r in range(1, regions):
                dual_total = dual_total + cbox[r, half : half + SUB, :]
            dual_total = jnp.sum(dual_total, axis=(0, 1), keepdims=True)
            weight = jnp.sqrt(
                weight * jnp.sqrt((dual_total + epsilon) / (primal_total + epsilon))
            )
            dual_step = step_scale * weight
        primal_step = step_scale / weight
        blocks = jnp.concatenate([cbox[r, :half, :] for r in range(regions)], axis=0)
        col_total = scatter(col_picks[...], blocks)
        before = x[...]
        moved = jnp.clip(before - primal_step * (cost[...] - col_total), 0.0, 1.0)
        x[...] = moved
        extrapolated[...] = (2.0 * moved - before).reshape(extrapolated.shape)
        if iteration == ITERS - 1:
            keep = pltpu.make_async_copy(x, primal_out, store_sem)
            keep.start()

        for s in range(SUB):
            primal_cols[s * chunks : (s + 1) * chunks, :] = extrapolated[cols_of[s]]
        routes = jnp.concatenate(
            [primal_cols[pl.ds(k, SUB, stride=chunks), :] for k in range(chunks)], axis=1
        )
        products = unstacked(
            lax.dot_general(
                stacked(routes), tiles[...], (((1,), (1,)), ((), ())),
                preferred_element_type=jnp.float32,
            )
        )
        own = jnp.where(sub == 0, products[:, :LANES], 0.0)
        for s in range(1, SUB):
            own = jnp.where(sub == s, products[:, s * LANES : (s + 1) * LANES], own)
        rbox[group, :SUB, :] = own
        rbox[group, SUB : 2 * SUB, :] = folded((moved - before) ** 2)
        rbox[group, 2 * SUB : 3 * SUB, :] = row_marks.astype(jnp.float32)
        exchange(group_copy, group, group_peers, rbox, rsend, rrecv)
        arrive(group_copy, group_peers, rbox, rsend, rrecv)

        if iteration == 0:
            span = row_picks.shape[1]
            piece = min(span, LANES)
            place = lax.broadcasted_iota(jnp.int32, (y.shape[0], piece), 0).astype(jnp.float32)
            spot = lax.broadcasted_iota(jnp.int32, (1, piece), 1)
            per = piece // SUB
            for j in range(span // piece):
                marks = rbox[j * per, 2 * SUB : 2 * SUB + 1, :piece]
                for i in range(1, per):
                    marks = jnp.where(
                        spot // SUB == i, rbox[j * per + i, 2 * SUB : 2 * SUB + 1, :piece], marks
                    )
                row_picks[:, j * piece : (j + 1) * piece] = jnp.where(
                    place == marks, 1.0, 0.0
                ).astype(jnp.bfloat16)
        blocks = jnp.concatenate([rbox[c, :SUB, :] for c in range(groups)], axis=0)
        coverage = scatter(row_picks[...], blocks)
        held = y[...]
        updated = held + dual_step * (1.0 - coverage)
        y[...] = updated
        dual_moves = folded((updated - held) ** 2)
        if iteration == ITERS - 1:
            last_box[region, :, :] = dual_moves
            exchange(region_copy, region, region_peers, last_box, last_send, last_recv)
            duals_out[...] = updated
        primal_total = rbox[0, SUB : 2 * SUB, :]
        for c in range(1, groups):
            primal_total = primal_total + rbox[c, SUB : 2 * SUB, :]
        primal_total = jnp.sum(primal_total, axis=(0, 1), keepdims=True)

    arrive(region_copy, region_peers, last_box, last_send, last_recv)
    dual_total = last_box[0]
    for r in range(1, regions):
        dual_total = dual_total + last_box[r]
    dual_total = jnp.sum(dual_total, axis=(0, 1), keepdims=True)
    balance_out[...] = jnp.sqrt(
        weight * jnp.sqrt((dual_total + epsilon) / (primal_total + epsilon))
    )
    for sent in pending:
        sent.wait_send()
    keep.wait()


def local(regions, groups, incidence, tile_rows, tile_cols, tile_count, route_cost, primal, duals, balance):
    slots, height, width = incidence.shape[2:]
    assert slots == SUB and height == LANES and width % LANES == 0
    chunks = width // LANES
    wide = (primal.shape[0] // LANES, LANES)
    tall = (duals.shape[0] // LANES, LANES)
    f32 = jnp.float32
    dma = pltpu.SemaphoreType.DMA
    smem = pl.BlockSpec(memory_space=pltpu.SMEM)
    vmem = pl.BlockSpec(memory_space=pltpu.VMEM)
    hbm = pl.BlockSpec(memory_space=pl.ANY)
    outs = pl.pallas_call(
        functools.partial(kernel, regions, groups),
        out_shape=(
            jax.ShapeDtypeStruct(wide, f32),
            jax.ShapeDtypeStruct(tall, f32),
            jax.ShapeDtypeStruct((1, 1), f32),
        ),
        in_specs=[smem] * 4 + [hbm] * 4,
        out_specs=(hbm, vmem, vmem),
        scratch_shapes=[
            pltpu.VMEM((slots * height, width), jnp.bfloat16),
            pltpu.VMEM(wide, f32),
            pltpu.VMEM(wide, f32),
            pltpu.VMEM(tall, f32),
            pltpu.VMEM((wide[0] // chunks, chunks, LANES), f32),
            pltpu.VMEM((SUB, LANES), f32),
            pltpu.VMEM((slots * chunks, LANES), f32),
            pltpu.VMEM((wide[0], regions * slots * chunks), jnp.bfloat16),
            pltpu.VMEM((tall[0], groups * slots), jnp.bfloat16),
            pltpu.VMEM((ITERS, regions, slots * chunks + SUB, LANES), f32),
            pltpu.VMEM((ITERS, groups, 3 * SUB, LANES), f32),
            pltpu.VMEM((regions, SUB, LANES), f32),
            dma((4,)),
            dma,
            dma((ITERS, regions)),
            dma((ITERS, regions)),
            dma((ITERS, groups)),
            dma((ITERS, groups)),
            dma((regions,)),
            dma((regions,)),
        ],
        compiler_params=pltpu.CompilerParams(
            collective_id=0, has_side_effects=True, vmem_limit_bytes=40 * 1024 * 1024
        ),
    )(
        tile_rows, tile_cols, tile_count, balance.reshape(1),
        incidence.reshape(slots * height, width),
        route_cost.reshape(wide), primal.reshape(wide), duals.reshape(tall),
    )
    return outs[0].reshape(-1), outs[1].reshape(-1), outs[2].reshape(())


def solution(mesh):
    return jax.shard_map(
        functools.partial(local, mesh.shape["region"], mesh.shape["cols"]),
        mesh=mesh,
        in_specs=(
            P("region", "cols", None, None, None),
            P("region", "cols", None),
            P("region", "cols", None),
            P("region", "cols"),
            P("cols"),
            P("cols"),
            P("region"),
            P(),
        ),
        out_specs=(P("cols"), P("region"), P()),
        check_vma=False,
    )
```

time: 182 us -> 40.5 us (0.22)
  blocking collectives: 90.1 us -> 0 us
  waiting for transfers between devices: 54.5 us -> 0 us
  Pallas kernels: 0 us -> 29.5 us
  between operations: 19.6 us -> 3.77 us
  matrix products: 6.67 us -> 0 us
  other arithmetic: 5.9 us -> 0 us
  local copies, waits for them, and re-layouts: 4.63 us -> 6.89 us
    psum x4 -> x0, blocking collectives: 90.1 us -> none  [the longest x2 77.2 us: local(): lax.psum(jnp.einsum('sr,si->ri', row_pick, products, precision=highest).r...]
    psum x2 -> x0, waiting for transfers between devices: 54.5 us -> none  [local(): col_total = lax.psum(col_terms, 'region')]
    pallas_call x0 -> x1, Pallas kernels: none -> 29.5 us  [local(): pl.pallas_call(functools.partial(kernel, regions, groups), out_shape=(jax...]
    dot_general x8 -> x0, matrix products: 6.67 us -> none  [the longest x2 3.44 us: local(): jnp.einsum('sij,sj->si', blocks, primal_cols, precision=highest, preferre...]
    unnamed x16 -> x14, local copies, waits for them, and re-layouts: 1.54 us -> 6.89 us
    reduce_sum x4 -> x0, other arithmetic: 5.16 us -> none  [the longest x2 3.25 us: local(): primal_moves = jnp.sum((moved - primal) ** 2)]
    gather x4 -> x0, local copies, waits for them, and re-layouts: 3 us -> none  [the longest x2 1.86 us: local(): dual_rows = duals.reshape(row_blocks, tile_height)[slot_rows]]
  transfers between devices with their start and end apart: 2 -> 0, of which waited for: 2 -> 0; matrix products, arithmetic and copies ran while one was open for 0% -> 0% of each run, Pallas kernels for 0% -> 0%
where the time goes in v1:
time: 40.5 us; the launch traced here: 40.2 us
  Pallas kernels  29.5 us (73%)
  local copies, waits for them, and re-layouts  6.89 us (17%)
  between operations  3.77 us (9%)
    pallas_call x1, Pallas kernels, local(): pl.pallas_call(functools.partial(kernel, regions, groups), out_shape=(jax...  29.5 us
    unnamed x14, local copies, waits for them, and re-layouts  6.89 us

profile of v1, /device:TPU:0, one launch (start us, length us, event | category | flops | bytes accessed | tf_op | source)
XLA Modules:
  0.0 40.2 jit_solution(18413800906979152670)
XLA Ops:
  1.9 0.0 copy-start
  1.9 1.6 %copy-done = bf16[1,1,8,128,1024]{4,3,2,1,0:T(8,128)(2,1)S(1)} copy-done((bf16[1,1,8,128,1024]{4,3,2,1,0:T(8,128)(2,1)S(1)}, bf16[1,1,8,128,1024]{4,3,2,1,0:T(8,128)(2,1)}, u32[]{:S(2)}) %copy-start) | copy-done | bytes 2097176
  3.5 0.0 copy-start.1
  3.5 0.9 %copy-done.1 = f32[65536]{0:T(1024)S(1)} copy-done((f32[65536]{0:T(1024)S(1)}, f32[65536]{0:T(1024)}, u32[]{:S(2)}) %copy-start.1) | copy-done | bytes 262168
  4.5 0.0 copy-start.2
  4.5 0.9 %copy-done.2 = f32[65536]{0:T(1024)S(1)} copy-done((f32[65536]{0:T(1024)S(1)}, f32[65536]{0:T(1024)}, u32[]{:S(2)}) %copy-start.2) | copy-done | bytes 262168
  5.4 0.0 copy-start.3
  5.4 0.8 %copy-done.3 = f32[8192]{0:T(1024)S(1)} copy-done((f32[8192]{0:T(1024)S(1)}, f32[8192]{0:T(1024)}, u32[]{:S(2)}) %copy-start.3) | copy-done | bytes 32792
  6.2 0.0 copy-start.4
  6.2 0.7 %copy-done.4 = s32[1,1,8]{2,1,0:T(1,128)S(1)} copy-done((s32[1,1,8]{2,1,0:T(1,128)S(1)}, s32[1,1,8]{2,1,0:T(1,128)}, u32[]{:S(2)}) %copy-start.4) | copy-done | bytes 56
  6.8 0.0 copy-start.5
  6.8 0.7 %copy-done.5 = s32[1,1,8]{2,1,0:T(1,128)S(1)} copy-done((s32[1,1,8]{2,1,0:T(1,128)S(1)}, s32[1,1,8]{2,1,0:T(1,128)}, u32[]{:S(2)}) %copy-start.5) | copy-done | bytes 56
  7.5 29.5 %shard_map.103 = (f32[512,128]{1,0:T(8,128)S(1)}, f32[64,128]{1,0:T(8,128)S(1)}, f32[1,1]{1,0:T(1,128)}) custom-call(s32[1,1,8]{2,1,0:T(1,128)S(1)} %copy-done.4, s32[1,1,8]{2,1,0:T(1,128)S(1)} %copy-done.5, s32[1,1]{1,0:T(1,128)S(6)} %copy.14.tile_count, f32[1]{0:T(128)} %bitcast.8.balance, bf16[1024,1024]{1,0:T(8,128)(2,1)S(1)} %bitcast.9, ...), custom_call_target="tpu_custom_call" | custom-call | tf_op jit(solution)/shard_map/pallas_call | solution.py:254
  37.0 0.7 %copy.16 = f32[65536]{0:T(1024)} copy(f32[65536]{0:T(1024)S(1)} %bitcast.12) | data formatting | bytes 524288
  37.7 0.6 %copy.17 = f32[8192]{0:T(1024)} copy(f32[8192]{0:T(1024)S(1)} %bitcast.14) | data formatting | bytes 65536
Async XLA Ops:
  1.9 1.6 %copy-start = (bf16[1,1,8,128,1024]{4,3,2,1,0:T(8,128)(2,1)S(1)}, bf16[1,1,8,128,1024]{4,3,2,1,0:T(8,128)(2,1)}, u32[]{:S(2)}) copy-start(bf16[1,1,8,128,1024]{4,3,2,1,0:T(8,128)(2,1)} %param.8) | copy-start | bytes 6291460
  3.5 0.9 %copy-start.1 = (f32[65536]{0:T(1024)S(1)}, f32[65536]{0:T(1024)}, u32[]{:S(2)}) copy-start(f32[65536]{0:T(1024)} %param.12) | copy-start | bytes 786436
  4.5 0.9 %copy-start.2 = (f32[65536]{0:T(1024)S(1)}, f32[65536]{0:T(1024)}, u32[]{:S(2)}) copy-start(f32[65536]{0:T(1024)} %param.13) | copy-start | bytes 786436
  5.4 0.8 %copy-start.3 = (f32[8192]{0:T(1024)S(1)}, f32[8192]{0:T(1024)}, u32[]{:S(2)}) copy-start(f32[8192]{0:T(1024)} %param.14) | copy-start | bytes 98308
  6.2 0.7 %copy-start.4 = (s32[1,1,8]{2,1,0:T(1,128)S(1)}, s32[1,1,8]{2,1,0:T(1,128)}, u32[]{:S(2)}) copy-start(s32[1,1,8]{2,1,0:T(1,128)} %tile_rows.1) | copy-start | bytes 100
  6.8 0.7 %copy-start.5 = (s32[1,1,8]{2,1,0:T(1,128)S(1)}, s32[1,1,8]{2,1,0:T(1,128)}, u32[]{:S(2)}) copy-start(s32[1,1,8]{2,1,0:T(1,128)} %tile_cols.1) | copy-start | bytes 100

commit v2 on v1

--- a/solution.py
+++ b/solution.py
@@ -42,16 +42,17 @@
 
 
 def folded(value):
-    return jnp.sum(value.reshape(-1, SUB, LANES), axis=0)
+    return jnp.sum(jnp.sum(value.reshape(-1, SUB, LANES), axis=0), axis=0, keepdims=True)
 
 
 def kernel(
     regions, groups,
-    tile_rows, tile_cols, tile_count, balance,
+    tile_rows_hbm, tile_cols_hbm, tile_count_hbm, balance_hbm,
     incidence_hbm, cost_hbm, primal_hbm, duals_hbm,
     primal_out, duals_out, balance_out,
+    tile_rows, tile_cols, tile_count, balance,
     tiles, cost, x, y, extrapolated, dual_rows, primal_cols,
-    col_picks, row_picks, col_box, row_box, last_box,
+    col_picks, row_picks, col_box, row_box, last_box, final_weight,
     load_sem, store_sem,
     col_send, col_recv, row_send, row_recv, last_send, last_recv,
 ):
@@ -62,10 +63,14 @@
     loads = [
         pltpu.make_async_copy(source, target, load_sem.at[i])
         for i, (source, target) in enumerate(
-            ((duals_hbm, y), (incidence_hbm, tiles), (primal_hbm, x), (cost_hbm, cost))
+            (
+                (duals_hbm, y), (incidence_hbm, tiles), (primal_hbm, x), (cost_hbm, cost),
+                (tile_rows_hbm, tile_rows), (tile_cols_hbm, tile_cols),
+                (tile_count_hbm, tile_count), (balance_hbm, balance),
+            )
         )
     ]
-    for load in loads:
+    for load in loads[4:] + loads[:4]:
         load.start()
 
     region_peers = [lax.rem(region + d, regions) for d in range(1, regions)]
@@ -102,6 +107,8 @@
         for slot, peer in enumerate(peers):
             copy(box, send, recv, peer, peer, slot).wait_recv()
 
+    for load in loads[4:]:
+        load.wait()
     lane = lax.broadcasted_iota(jnp.int32, (SUB, LANES), 1)
     sub = lax.broadcasted_iota(jnp.int32, (SUB, LANES), 0)
     rows_of, cols_of = [], []
@@ -114,9 +121,8 @@
         col_marks = jnp.where(mine, cols_of[s] * chunks + (lane // SUB) % chunks, col_marks)
         row_marks = jnp.where(mine, rows_of[s], row_marks)
 
-    weight = jnp.full((1, 1), balance[0], jnp.float32)
+    weight = jnp.full((1, 1), balance[0, 0], jnp.float32)
     half = SUB * chunks
-    pl.semaphore_wait(barrier, regions + groups - 2)
 
     for iteration in range(ITERS):
         cbox, csend, crecv = col_box.at[iteration], col_send.at[iteration], col_recv.at[iteration]
@@ -134,12 +140,14 @@
         products = unstacked(
             jnp.dot(stacked(diagonal), tiles[...], preferred_element_type=jnp.float32)
         )
+        if iteration == 0:
+            pl.semaphore_wait(barrier, regions + groups - 2)
         for k in range(chunks):
             cbox[region, k * SUB : (k + 1) * SUB, :] = products[:, k * LANES : (k + 1) * LANES]
         if iteration == 0:
-            cbox[region, half : half + SUB, :] = col_marks.astype(jnp.float32)
+            cbox[region, half : half + 1, :] = col_marks[:1].astype(jnp.float32)
         else:
-            cbox[region, half : half + SUB, :] = dual_moves
+            cbox[region, half : half + 1, :] = dual_moves
         exchange(region_copy, region, region_peers, cbox, csend, crecv)
         if iteration == 0:
             loads[2].wait()
@@ -158,9 +166,9 @@
                     place == marks, 1.0, 0.0
                 ).astype(jnp.bfloat16)
         else:
-            dual_total = cbox[0, half : half + SUB, :]
+            dual_total = cbox[0, half : half + 1, :]
             for r in range(1, regions):
-                dual_total = dual_total + cbox[r, half : half + SUB, :]
+                dual_total = dual_total + cbox[r, half : half + 1, :]
             dual_total = jnp.sum(dual_total, axis=(0, 1), keepdims=True)
             weight = jnp.sqrt(
                 weight * jnp.sqrt((dual_total + epsilon) / (primal_total + epsilon))
@@ -174,8 +182,8 @@
         x[...] = moved
         extrapolated[...] = (2.0 * moved - before).reshape(extrapolated.shape)
         if iteration == ITERS - 1:
-            keep = pltpu.make_async_copy(x, primal_out, store_sem)
-            keep.start()
+            stores = [pltpu.make_async_copy(x, primal_out, store_sem.at[0])]
+            stores[0].start()
 
         for s in range(SUB):
             primal_cols[s * chunks : (s + 1) * chunks, :] = extrapolated[cols_of[s]]
@@ -192,8 +200,8 @@
         for s in range(1, SUB):
             own = jnp.where(sub == s, products[:, s * LANES : (s + 1) * LANES], own)
         rbox[group, :SUB, :] = own
-        rbox[group, SUB : 2 * SUB, :] = folded((moved - before) ** 2)
-        rbox[group, 2 * SUB : 3 * SUB, :] = row_marks.astype(jnp.float32)
+        rbox[group, SUB : SUB + 1, :] = folded((moved - before) ** 2)
+        rbox[group, SUB + 1 : SUB + 2, :] = row_marks[:1].astype(jnp.float32)
         exchange(group_copy, group, group_peers, rbox, rsend, rrecv)
         arrive(group_copy, group_peers, rbox, rsend, rrecv)
 
@@ -204,10 +212,10 @@
             spot = lax.broadcasted_iota(jnp.int32, (1, piece), 1)
             per = piece // SUB
             for j in range(span // piece):
-                marks = rbox[j * per, 2 * SUB : 2 * SUB + 1, :piece]
+                marks = rbox[j * per, SUB + 1 : SUB + 2, :piece]
                 for i in range(1, per):
                     marks = jnp.where(
-                        spot // SUB == i, rbox[j * per + i, 2 * SUB : 2 * SUB + 1, :piece], marks
+                        spot // SUB == i, rbox[j * per + i, SUB + 1 : SUB + 2, :piece], marks
                     )
                 row_picks[:, j * piece : (j + 1) * piece] = jnp.where(
                     place == marks, 1.0, 0.0
@@ -221,10 +229,11 @@
         if iteration == ITERS - 1:
             last_box[region, :, :] = dual_moves
             exchange(region_copy, region, region_peers, last_box, last_send, last_recv)
-            duals_out[...] = updated
-        primal_total = rbox[0, SUB : 2 * SUB, :]
+            stores.append(pltpu.make_async_copy(y, duals_out, store_sem.at[1]))
+            stores[1].start()
+        primal_total = rbox[0, SUB : SUB + 1, :]
         for c in range(1, groups):
-            primal_total = primal_total + rbox[c, SUB : 2 * SUB, :]
+            primal_total = primal_total + rbox[c, SUB : SUB + 1, :]
         primal_total = jnp.sum(primal_total, axis=(0, 1), keepdims=True)
 
     arrive(region_copy, region_peers, last_box, last_send, last_recv)
@@ -232,12 +241,20 @@
     for r in range(1, regions):
         dual_total = dual_total + last_box[r]
     dual_total = jnp.sum(dual_total, axis=(0, 1), keepdims=True)
-    balance_out[...] = jnp.sqrt(
+    final_weight[...] = jnp.sqrt(
         weight * jnp.sqrt((dual_total + epsilon) / (primal_total + epsilon))
     )
+    stores.append(pltpu.make_async_copy(final_weight, balance_out, store_sem.at[2]))
+    stores[2].start()
     for sent in pending:
         sent.wait_send()
-    keep.wait()
+    for store in stores:
+        store.wait()
+
+
+def handed_over(*refs):
+    for i in range(3):
+        refs[3 + i][...] = refs[i][...]
 
 
 def local(regions, groups, incidence, tile_rows, tile_cols, tile_count, route_cost, primal, duals, balance):
@@ -248,9 +265,7 @@
     tall = (duals.shape[0] // LANES, LANES)
     f32 = jnp.float32
     dma = pltpu.SemaphoreType.DMA
-    smem = pl.BlockSpec(memory_space=pltpu.SMEM)
-    vmem = pl.BlockSpec(memory_space=pltpu.VMEM)
-    hbm = pl.BlockSpec(memory_space=pl.ANY)
+    hbm = pl.BlockSpec(memory_space=pltpu.HBM)
     outs = pl.pallas_call(
         functools.partial(kernel, regions, groups),
         out_shape=(
@@ -258,9 +273,13 @@
             jax.ShapeDtypeStruct(tall, f32),
             jax.ShapeDtypeStruct((1, 1), f32),
         ),
-        in_specs=[smem] * 4 + [hbm] * 4,
-        out_specs=(hbm, vmem, vmem),
+        in_specs=[hbm] * 8,
+        out_specs=(hbm, hbm, hbm),
         scratch_shapes=[
+            pltpu.SMEM(tile_rows.shape, jnp.int32),
+            pltpu.SMEM(tile_cols.shape, jnp.int32),
+            pltpu.SMEM(tile_count.shape, jnp.int32),
+            pltpu.SMEM((1, 1), f32),
             pltpu.VMEM((slots * height, width), jnp.bfloat16),
             pltpu.VMEM(wide, f32),
             pltpu.VMEM(wide, f32),
@@ -270,11 +289,12 @@
             pltpu.VMEM((slots * chunks, LANES), f32),
             pltpu.VMEM((wide[0], regions * slots * chunks), jnp.bfloat16),
             pltpu.VMEM((tall[0], groups * slots), jnp.bfloat16),
-            pltpu.VMEM((ITERS, regions, slots * chunks + SUB, LANES), f32),
-            pltpu.VMEM((ITERS, groups, 3 * SUB, LANES), f32),
-            pltpu.VMEM((regions, SUB, LANES), f32),
-            dma((4,)),
-            dma,
+            pltpu.VMEM((ITERS, regions, slots * chunks + 1, LANES), f32),
+            pltpu.VMEM((ITERS, groups, SUB + 2, LANES), f32),
+            pltpu.VMEM((regions, 1, LANES), f32),
+            pltpu.VMEM((1, 1), f32),
+            dma((8,)),
+            dma((3,)),
             dma((ITERS, regions)),
             dma((ITERS, regions)),
             dma((ITERS, groups)),
@@ -283,13 +303,17 @@
             dma((regions,)),
         ],
         compiler_params=pltpu.CompilerParams(
-            collective_id=0, has_side_effects=True, vmem_limit_bytes=40 * 1024 * 1024
+            collective_id=0, has_side_effects=True, vmem_limit_bytes=56 * 1024 * 1024
         ),
     )(
-        tile_rows, tile_cols, tile_count, balance.reshape(1),
+        tile_rows, tile_cols, tile_count, balance.reshape(1, 1),
         incidence.reshape(slots * height, width),
         route_cost.reshape(wide), primal.reshape(wide), duals.reshape(tall),
     )
+    outs = pl.pallas_call(
+        handed_over,
+        out_shape=tuple(jax.ShapeDtypeStruct(out.shape, f32) for out in outs),
+    )(*outs)
     return outs[0].reshape(-1), outs[1].reshape(-1), outs[2].reshape(())
 
 

time: 40.5 us -> 31.7 us (0.78)
  local copies, waits for them, and re-layouts: 6.89 us -> 0 us
  between operations: 3.77 us -> 1.93 us
    unnamed x14 -> x0, local copies, waits for them, and re-layouts: 6.89 us -> none
    pallas_call x0 -> x1, Pallas kernels: none -> 2.37 us  [local(): pl.pallas_call(handed_over, out_shape=tuple((jax.ShapeDtypeStruct(out.sha...]
    pallas_call x1, Pallas kernels: 29.5 us -> 27.2 us  [local(): pl.pallas_call(functools.partial(kernel, regions, groups), out_shape=(jax...]
where the time goes in v2:
time: 31.7 us; the launch traced here: 31.5 us
  Pallas kernels  29.6 us (93%)
  between operations  1.93 us (6%)
    pallas_call x1, Pallas kernels, local(): pl.pallas_call(functools.partial(kernel, regions, groups), out_shape=(jax...  27.2 us
    pallas_call x1, Pallas kernels, local(): pl.pallas_call(handed_over, out_shape=tuple((jax.ShapeDtypeStruct(out.sha...  2.37 us

profile of v2, /device:TPU:0, one launch (start us, length us, event | category | flops | bytes accessed | tf_op | source)
XLA Modules:
  0.0 31.5 jit_solution(12266266464619924558)
XLA Ops:
  1.9 27.2 %shard_map.103 = (f32[512,128]{1,0:T(8,128)}, f32[64,128]{1,0:T(8,128)}, f32[1,1]{1,0:T(1,128)}) custom-call(s32[1,1,8]{2,1,0:T(1,128)} %tile_rows_hbm.1, s32[1,1,8]{2,1,0:T(1,128)} %tile_cols_hbm.1, s32[1,1]{1,0:T(1,128)S(6)} %copy.11.tile_count_hbm, f32[1,1]{1,0:T(1,128)} %bitcast.8.balance_hbm, bf16[1024,1024]{1,0:T(8,128)(2,1)} %bitcast.9, ...), custom_call_target="tpu_custom_call" | custom-call | tf_op jit(solution)/shard_map/pallas_call | solution.py:269
  29.1 2.4 %shard_map.104 = (f32[512,128]{1,0:T(8,128)}, f32[64,128]{1,0:T(8,128)}, f32[1,1]{1,0:T(1,128)}) custom-call(f32[512,128]{1,0:T(8,128)} %get-tuple-element.9.refs_0_, f32[64,128]{1,0:T(8,128)} %get-tuple-element.10.refs_1_, f32[1,1]{1,0:T(1,128)} %get-tuple-element.11.refs_2_), custom_call_target="tpu_custom_call" | custom-call | tf_op jit(solution)/shard_map/pallas_call | solution.py:313

commit v3 on v2

--- a/solution.py
+++ b/solution.py
@@ -60,6 +60,14 @@
     width = tiles.shape[1]
     chunks = width // LANES
 
+    region_peers = [lax.rem(region + d, regions) for d in range(1, regions)]
+    group_peers = [lax.rem(group + d, groups) for d in range(1, groups)]
+    barrier = pltpu.get_barrier_semaphore()
+    for peer in region_peers:
+        pl.semaphore_signal(barrier, inc=1, device_id=(peer, group), device_id_type=MESH)
+    for peer in group_peers:
+        pl.semaphore_signal(barrier, inc=1, device_id=(region, peer), device_id_type=MESH)
+
     loads = [
         pltpu.make_async_copy(source, target, load_sem.at[i])
         for i, (source, target) in enumerate(
@@ -72,14 +80,6 @@
     ]
     for load in loads[4:] + loads[:4]:
         load.start()
-
-    region_peers = [lax.rem(region + d, regions) for d in range(1, regions)]
-    group_peers = [lax.rem(group + d, groups) for d in range(1, groups)]
-    barrier = pltpu.get_barrier_semaphore()
-    for peer in region_peers:
-        pl.semaphore_signal(barrier, inc=1, device_id=(peer, group), device_id_type=MESH)
-    for peer in group_peers:
-        pl.semaphore_signal(barrier, inc=1, device_id=(region, peer), device_id_type=MESH)
 
     def region_copy(box, send, recv, owner, peer, send_slot):
         return pltpu.make_async_remote_copy(
@@ -252,11 +252,6 @@
         store.wait()
 
 
-def handed_over(*refs):
-    for i in range(3):
-        refs[3 + i][...] = refs[i][...]
-
-
 def local(regions, groups, incidence, tile_rows, tile_cols, tile_count, route_cost, primal, duals, balance):
     slots, height, width = incidence.shape[2:]
     assert slots == SUB and height == LANES and width % LANES == 0
@@ -269,12 +264,12 @@
     outs = pl.pallas_call(
         functools.partial(kernel, regions, groups),
         out_shape=(
-            jax.ShapeDtypeStruct(wide, f32),
-            jax.ShapeDtypeStruct(tall, f32),
-            jax.ShapeDtypeStruct((1, 1), f32),
+            pltpu.VMEM(wide, f32),
+            pltpu.VMEM(tall, f32),
+            pltpu.VMEM((1, 1), f32),
         ),
         in_specs=[hbm] * 8,
-        out_specs=(hbm, hbm, hbm),
+        out_specs=(pl.BlockSpec(memory_space=pl.ANY),) * 3,
         scratch_shapes=[
             pltpu.SMEM(tile_rows.shape, jnp.int32),
             pltpu.SMEM(tile_cols.shape, jnp.int32),
@@ -310,10 +305,6 @@
         incidence.reshape(slots * height, width),
         route_cost.reshape(wide), primal.reshape(wide), duals.reshape(tall),
     )
-    outs = pl.pallas_call(
-        handed_over,
-        out_shape=tuple(jax.ShapeDtypeStruct(out.shape, f32) for out in outs),
-    )(*outs)
     return outs[0].reshape(-1), outs[1].reshape(-1), outs[2].reshape(())
 
 

time: 31.7 us -> 31.3 us (0.987)
  Pallas kernels: 29.6 us -> 26.7 us
  local copies, waits for them, and re-layouts: 0 us -> 1.34 us
  between operations: 1.93 us -> 3.1 us
    pallas_call x2 -> x1, Pallas kernels: 29.6 us -> 26.7 us  [local(): pl.pallas_call(functools.partial(kernel, regions, groups), out_shape=(plt...]
    unnamed x0 -> x2, local copies, waits for them, and re-layouts: none -> 1.34 us
where the time goes in v3:
time: 31.3 us; the launch traced here: 31.2 us
  Pallas kernels  26.7 us (85%)
  between operations  3.1 us (10%)
  local copies, waits for them, and re-layouts  1.34 us (4%)
    pallas_call x1, Pallas kernels, local(): pl.pallas_call(functools.partial(kernel, regions, groups), out_shape=(plt...  26.7 us
    unnamed x2, local copies, waits for them, and re-layouts  1.34 us

profile of v3, /device:TPU:0, one launch (start us, length us, event | category | flops | bytes accessed | tf_op | source)
XLA Modules:
  0.0 31.2 jit_solution(10760817086286072435)
XLA Ops:
  1.9 26.7 %shard_map.103 = (f32[512,128]{1,0:T(8,128)S(1)}, f32[64,128]{1,0:T(8,128)S(1)}, f32[1,1]{1,0:T(1,128)S(1)}) custom-call(s32[1,1,8]{2,1,0:T(1,128)} %tile_rows_hbm.1, s32[1,1,8]{2,1,0:T(1,128)} %tile_cols_hbm.1, s32[1,1]{1,0:T(1,128)S(6)} %copy.17.tile_count_hbm, f32[1,1]{1,0:T(1,128)} %bitcast.8.balance_hbm, bf16[1024,1024]{1,0:T(8,128)(2,1)} %bitcast.11, ...), custom_call_target="tpu_custom_call" | custom-call | tf_op jit(solution)/shard_map/pallas_call | solution.py:264
  28.7 0.7 %copy.14 = f32[65536]{0:T(1024)} copy(f32[65536]{0:T(1024)S(1)} %bitcast.9) | data formatting | bytes 524288
  29.4 0.6 %copy.15 = f32[8192]{0:T(1024)} copy(f32[8192]{0:T(1024)S(1)} %bitcast.10) | data formatting | bytes 65536
